TPU v7x, 128 devices: a whole 4x4x4 slice. The times are simulated.
128 devices in a mesh: gx: 8 (over x, core), gy: 16 (over y, z).
Axes of the slice: x: 4, y: 4, z: 4, core: 2. Of those that a mesh axis runs over, the one named last changes fastest.
Arguments:
- adjoint_state: float32 [192, 256, 4096], P(None, 'gx', 'gy'), may hold values from -6 to 6
- inverse_scale: float32 [256, 4096], P('gx', 'gy'), may hold values from 0.35 to 1.2
- element_inverse: float32 [192, 192], replicated, may hold values from -0.4375 to 0.4375
- trace_op: float32 [96, 192], replicated, may hold values from -0.4375 to 0.4375
- lift_op: float32 [192, 96], replicated, may hold values from -0.625 to 0.625
- obs_elem: int32 [2, 98304], P(None, ('gx', 'gy')), may hold values from 0 to 1048575, as said below
- obs_count: int32 [2, 128], P(None, ('gx', 'gy')), may hold values from 6 to 768, as said below
- obs_basis: float32 [2, 64, 98304], P(None, None, ('gx', 'gy')), may hold values from -5 to 5
- innovation: float32 [2, 98304], P(None, ('gx', 'gy')), may hold values from -5 to 5
Outputs:
- adjoint_out: float32 [192, 256, 4096], P(None, 'gx', 'gy')
Inputs may be any that keep to these rules, and one draw needn't show every extreme that they name: `obs_elem`: among the live observations of one device in one step, at most 6 lie in elements of any one device; in every step the first 6 slots of each device are live and all lie in elements of one device. `obs_count`: device 0 has all 768 slots live in every step.
All inputs are finite; a program needn't handle non-finite values.
Results may differ from a plain program's by a relative error of at most 0.0001.
Values sent between devices are 32-bit elements; how exact they have to be, the bound alone decides.
A program may use at most 128 MiB of HBM per device.

v0:
```python
import functools

import jax
import jax.numpy as jnp
from jax import lax
from jax.experimental import pallas as pl
from jax.experimental.pallas import tpu as pltpu
from jax.sharding import PartitionSpec as P

F32 = jnp.float32
BF = jnp.bfloat16
MESH = pl.DeviceIdType.MESH
STEPS = 2
NODES = 64
FN = 24
STATE = 192
EX = 32
EY = 256
OBS = 768
CAP = 6
GX = 8
GY = 16
DEV = GX * GY
VMEM = pl.BlockSpec(memory_space=pltpu.VMEM)
SMEM = pl.BlockSpec(memory_space=pltpu.SMEM)
ANY = pl.BlockSpec(memory_space=pl.ANY)


def dot(a, b):
    return jnp.dot(a, b, preferred_element_type=F32)


def dot_nt(a, b):
    return lax.dot_general(a, b, (((1,), (1,)), ((), ())), preferred_element_type=F32)


def dot_full(a, b):
    return jnp.dot(a, b, preferred_element_type=F32, precision=lax.Precision.HIGHEST)


def split(v):
    hi = v.astype(BF)
    return hi, (v - hi.astype(F32)).astype(BF)


def iota(shape, dim):
    return lax.broadcasted_iota(jnp.int32, shape, dim)


def pack(elem_ref, count_ref, basis_ref, innov_ref, out_ref):
    lane = iota((1, OBS), 1)
    owner = iota((DEV, OBS), 0)
    tri = (iota((256, 256), 0) < iota((256, 256), 1)).astype(F32).astype(BF)
    row = iota((128, OBS), 0)
    halves = []
    ids = jnp.zeros((DEV, 128), F32)
    for s in range(STEPS):
        elem = elem_ref[s : s + 1, :]
        gx = lax.shift_right_logical(elem, 17)
        lx = lax.shift_right_logical(elem, 12) & (EX - 1)
        gy = lax.shift_right_logical(elem, 8) & (GY - 1)
        ly = elem & (EY - 1)
        live = lane < count_ref[s, 0]
        target = jnp.where(live, gx * GY + gy, -1)
        member = (owner == target).astype(F32)
        carry = jnp.zeros((DEV, 1), F32)
        running = []
        for b in range(OBS // 256):
            part = member[:, b * 256 : (b + 1) * 256]
            running.append(dot(part.astype(BF), tri) + carry)
            carry = carry + jnp.sum(part, axis=1, keepdims=True)
        before = jnp.concatenate(running, axis=1)
        rank = jnp.sum(member * before, axis=0, keepdims=True).astype(jnp.int32)
        hi, lo = split(basis_ref[s] * innov_ref[s : s + 1, :])
        both = jnp.concatenate([hi, lo], axis=0)
        picked = []
        for j in range(CAP):
            chosen = jnp.where(rank == j, member, 0.0).astype(BF)
            got = dot_nt(chosen, both)
            picked.append(got + pltpu.roll(got, 64, 1))
        halves.append(picked)
        where = jnp.where(row == rank + 16 * s, lx + 1, 0)
        where = where + jnp.where(row == rank + 16 * s + 8, ly, 0)
        ids = ids + dot_nt(member.astype(BF), where.astype(F32).astype(BF))
    low = iota((DEV, 128), 1) < 64
    for j in range(CAP):
        out_ref[pl.ds(j, DEV, stride=8), :] = jnp.where(low, halves[0][j], halves[1][j])
    out_ref[pl.ds(CAP, DEV, stride=8), :] = ids
    out_ref[pl.ds(CAP + 1, DEV, stride=8), :] = jnp.zeros((DEV, 128), F32)


def route_kernel(elem_ref, count_ref, basis_ref, innov_ref, got_ref, out_ref, send_sem, recv_sem):
    px, py = lax.axis_index("gx"), lax.axis_index("gy")
    me = px * GY + py
    barrier = pltpu.get_barrier_semaphore()

    def greet(k, carry):
        peer = (me + k) % DEV
        pl.semaphore_signal(
            barrier, inc=1, device_id=(peer // GY, peer % GY), device_id_type=MESH
        )
        return carry

    lax.fori_loop(1, DEV, greet, 0)
    pack(elem_ref, count_ref, basis_ref, innov_ref, out_ref)
    pl.semaphore_wait(barrier, DEV - 1)
    mine = pl.ds(pl.multiple_of(me * 8, 8), 8)

    def send(k, carry):
        peer = (me + k) % DEV
        pltpu.make_async_remote_copy(
            src_ref=out_ref.at[pl.ds(pl.multiple_of(peer * 8, 8), 8)],
            dst_ref=got_ref.at[mine],
            send_sem=send_sem,
            recv_sem=recv_sem,
            device_id=(peer // GY, peer % GY),
            device_id_type=MESH,
        ).start()
        return carry

    lax.fori_loop(1, DEV, send, 0)
    got_ref[mine, :] = out_ref[mine, :]
    rest = pl.ds(0, (DEV - 1) * 8)
    pltpu.make_async_copy(out_ref.at[rest], out_ref.at[rest], send_sem).wait()
    pltpu.make_async_copy(got_ref.at[rest], got_ref.at[rest], recv_sem).wait()


def route(obs_elem, obs_count, obs_basis, innovation):
    return pl.pallas_call(
        route_kernel,
        out_shape=pltpu.VMEM((DEV * 8, 128), F32),
        in_specs=[VMEM, SMEM, VMEM, VMEM],
        out_specs=VMEM,
        scratch_shapes=[
            pltpu.VMEM((DEV * 8, 128), F32),
            pltpu.SemaphoreType.DMA,
            pltpu.SemaphoreType.DMA,
        ],
        compiler_params=pltpu.CompilerParams(
            collective_id=0, has_side_effects=True, vmem_limit_bytes=24 << 20
        ),
        name="route",
    )(obs_elem, obs_count, obs_basis, innovation)


def unpack(got_ref, pay_ref, col_ref, rowid_ref):
    ids = got_ref[pl.ds(CAP, DEV, stride=8), :].T
    parts = [got_ref[pl.ds(j, DEV, stride=8), :].T for j in range(CAP)]
    for s in range(STEPS):
        values = jnp.concatenate([p[s * 64 : s * 64 + 64] for p in parts], axis=1)
        hi, lo = split(values)
        pay_ref[s, 0:64, :] = hi
        pay_ref[s, 64:128, :] = lo
        xs = [ids[s * 16 + j : s * 16 + j + 1, :] for j in range(CAP)]
        ys = [ids[s * 16 + 8 + j : s * 16 + 9 + j, :] for j in range(CAP)]
        rowid_ref[s : s + 1, :] = jnp.concatenate(xs, axis=1).astype(jnp.int32) - 1
        ycol = jnp.concatenate(ys, axis=1).astype(jnp.int32)
        hot = (iota((EY, OBS), 0) == ycol).astype(F32)
        col_ref[s] = hot.T.astype(BF)


def force(s, pay_ref, col_ref, rowid_ref, force_ref):
    group = 4

    def body(g, carry):
        rowid = rowid_ref[s : s + 1, :]
        pay = pay_ref[s]
        stack = []
        for i in range(group):
            here = (rowid == g * group + i).astype(F32).astype(BF)
            stack.append(pay * here)
        got = dot(jnp.concatenate(stack, axis=0), col_ref[s])
        for i in range(group):
            top = got[i * 128 : i * 128 + 64]
            force_ref[s, g * group + i] = top + got[i * 128 + 64 : i * 128 + 128]
        return carry

    lax.fori_loop(0, EX // group, body, 0)


def order(i):
    return jnp.where(i == 0, 0, jnp.where(i == 1, EX - 1, i - 1))


def traces(x, state, t_ref, near_ref, carry):
    down, up = carry
    hi, lo = state
    tr = dot(t_ref[0], hi) + dot(t_ref[1], hi) + dot(t_ref[0], lo)
    west, east = tr[0:FN], tr[FN : 2 * FN]
    south, north = tr[2 * FN : 3 * FN], tr[3 * FN : 4 * FN]
    near_ref[x, FN : 2 * FN, :] = west
    near_ref[x + 2, 0:FN, :] = east
    from_south = pltpu.roll(north, 1, 1)
    from_north = pltpu.roll(south, EY - 1, 1)
    near_ref[x + 1, 2 * FN : 3 * FN, :] = from_south
    near_ref[x + 1, 3 * FN : 4 * FN, :] = from_north
    here = iota((FN, 128), 1) == x
    up = jnp.where(here, from_south[:, 0:1], up)
    down = jnp.where(here, from_north[:, EY - 1 : EY], down)
    return down, up


def patch(near_ref, below, above):
    first = iota((FN, 128), 1) == 0
    last = iota((FN, 128), 1) == 127

    def body(x, carry):
        low = pltpu.roll(below, (128 - x) % 128, 1)
        high = pltpu.roll(above, 127 - x, 1)
        s_rows, n_rows = slice(2 * FN, 3 * FN), slice(3 * FN, 4 * FN)
        near_ref[x + 1, s_rows, 0:128] = jnp.where(first, low, near_ref[x + 1, s_rows, 0:128])
        near_ref[x + 1, n_rows, 128:256] = jnp.where(
            last, high, near_ref[x + 1, n_rows, 128:256]
        )
        return carry

    lax.fori_loop(0, EX, body, 0, unroll=2)


def finish(x, acc_ref, near_ref, b_ref, scale_ref):
    hi, lo = split(near_ref[x + 1])
    lifted = dot(b_ref[0], hi) + dot(b_ref[1], hi) + dot(b_ref[0], lo)
    return (acc_ref[x] + lifted) * scale_ref[pl.ds(x, 1), :]


def steps_kernel(
    state_ref, scale_ref, inverse_ref, trace_ref, lift_ref, got_ref,
    acc_ref, near2_ref, b_ref,
    stage, slab, near1_ref, force_ref, pay_ref, col_ref, rowid_ref, a_ref, t_ref,
    ysend, yrecv, load_sem, send_sem, recv_sem,
):
    px, py = lax.axis_index("gx"), lax.axis_index("gy")
    peers = (
        (lax.rem(px + GX - 1, GX), py),
        (lax.rem(px + 1, GX), py),
        (px, lax.rem(py + GY - 1, GY)),
        (px, lax.rem(py + 1, GY)),
    )
    loads = []
    for c in range(EX // 8):
        for h in range(2):
            loads.append(
                pltpu.make_async_copy(
                    state_ref.at[:, c * 8 : c * 8 + 8, h * 128 : h * 128 + 128],
                    stage.at[c, h],
                    load_sem.at[c, h],
                )
            )
            loads[-1].start()
    barrier = pltpu.get_barrier_semaphore()
    for peer in peers:
        pl.semaphore_signal(barrier, inc=1, device_id=peer, device_id_type=MESH)

    operator = trace_ref[...]
    inverse = inverse_ref[...]
    half = 0.5 * dot_full(inverse, lift_ref[...])
    whole = inverse + dot_full(half, operator)
    for ref, value in ((a_ref, whole), (b_ref, half), (t_ref, operator)):
        hi, lo = split(value)
        ref[0] = hi
        ref[1] = lo
    unpack(got_ref, pay_ref, col_ref, rowid_ref)
    for s in range(STEPS):
        force(s, pay_ref, col_ref, rowid_ref, force_ref)
    for copy in loads:
        copy.wait()
    pl.semaphore_wait(barrier, 4)

    def send_halos(s, near_ref, down, up):
        ysend[s, 0] = down
        ysend[s, 1] = up
        pairs = (
            (near_ref.at[0, FN : 2 * FN], near_ref.at[EX, FN : 2 * FN]),
            (near_ref.at[EX + 1, 0:FN], near_ref.at[1, 0:FN]),
            (ysend.at[s, 0], yrecv.at[s, 1]),
            (ysend.at[s, 1], yrecv.at[s, 0]),
        )
        copies = []
        for k in range(4):
            copies.append(
                pltpu.make_async_remote_copy(
                    src_ref=pairs[k][0],
                    dst_ref=pairs[k][1],
                    send_sem=send_sem.at[s, k],
                    recv_sem=recv_sem.at[s, k],
                    device_id=peers[k],
                    device_id_type=MESH,
                )
            )
            copies[-1].start()
        return copies

    def take_halos(s, near_ref, copies):
        for copy in copies:
            copy.wait()
        below = jnp.where(py == 0, ysend[s, 0], yrecv[s, 0])
        above = jnp.where(py == GY - 1, ysend[s, 1], yrecv[s, 1])
        patch(near_ref, below, above)

    def keep(x, s, value, near_ref, carry):
        value = jnp.concatenate([value[0:NODES] + force_ref[s, x], value[NODES:STATE]], axis=0)
        hi, lo = split(value)
        slab[x, 0] = hi
        slab[x, 1] = lo
        return traces(x, (hi, lo), t_ref, near_ref, carry)

    def first(i, carry):
        x = order(i)
        c, r = x // 8, x % 8
        halves = [stage[c, h, :, pl.ds(r, 1), :].reshape(STATE, 128) for h in range(2)]
        return keep(x, 0, jnp.concatenate(halves, axis=1), near1_ref, carry)

    def middle(i, carry):
        x = order(i)
        return keep(x, 1, finish(x, acc_ref, near1_ref, b_ref, scale_ref), near2_ref, carry)

    def hold(x, carry):
        hi, lo = slab[x, 0], slab[x, 1]
        acc_ref[x] = dot(a_ref[0], hi) + dot(a_ref[1], hi) + dot(a_ref[0], lo)
        return carry

    rim = jnp.zeros((FN, 128), F32)
    down, up = lax.fori_loop(0, EX, first, (rim, rim), unroll=2)
    copies = send_halos(0, near1_ref, down, up)
    lax.fori_loop(0, EX, hold, 0, unroll=2)
    take_halos(0, near1_ref, copies)
    down, up = lax.fori_loop(0, EX, middle, (rim, rim), unroll=2)
    copies = send_halos(1, near2_ref, down, up)
    lax.fori_loop(0, EX, hold, 0, unroll=2)
    take_halos(1, near2_ref, copies)


def steps(state, scale, inverse, trace, lift, got):
    return pl.pallas_call(
        steps_kernel,
        out_shape=(
            pltpu.VMEM((EX, STATE, EY), F32),
            pltpu.VMEM((EX + 2, 4 * FN, EY), F32),
            pltpu.VMEM((2, STATE, 4 * FN), BF),
        ),
        in_specs=[ANY, VMEM, VMEM, VMEM, VMEM, VMEM],
        out_specs=(VMEM, VMEM, VMEM),
        scratch_shapes=[
            pltpu.VMEM((EX // 8, 2, STATE, 8, 128), F32),
            pltpu.VMEM((EX, 2, STATE, EY), BF),
            pltpu.VMEM((EX + 2, 4 * FN, EY), F32),
            pltpu.VMEM((STEPS, EX, NODES, EY), F32),
            pltpu.VMEM((STEPS, 128, OBS), BF),
            pltpu.VMEM((STEPS, OBS, EY), BF),
            pltpu.VMEM((8, OBS), jnp.int32),
            pltpu.VMEM((2, STATE, STATE), BF),
            pltpu.VMEM((2, 4 * FN, STATE), BF),
            pltpu.VMEM((STEPS, 2, FN, 128), F32),
            pltpu.VMEM((STEPS, 2, FN, 128), F32),
            pltpu.SemaphoreType.DMA((EX // 8, 2)),
            pltpu.SemaphoreType.DMA((STEPS, 4)),
            pltpu.SemaphoreType.DMA((STEPS, 4)),
        ],
        compiler_params=pltpu.CompilerParams(
            collective_id=1, has_side_effects=True, vmem_limit_bytes=40 << 20
        ),
        name="steps",
    )(state, scale, inverse, trace, lift, got)


def last_kernel(acc_ref, near_ref, b_ref, scale_ref, out_ref, stage, sem):
    copies = []
    for c in range(EX // 8):

        def body(r, carry):
            x = c * 8 + r
            value = finish(x, acc_ref, near_ref, b_ref, scale_ref)
            for h in range(2):
                stage[c, h, :, pl.ds(r, 1), :] = value[:, h * 128 : h * 128 + 128].reshape(
                    STATE, 1, 128
                )
            return carry

        lax.fori_loop(0, 8, body, 0, unroll=2)
        for h in range(2):
            copies.append(
                pltpu.make_async_copy(
                    stage.at[c, h],
                    out_ref.at[:, c * 8 : c * 8 + 8, h * 128 : h * 128 + 128],
                    sem.at[c, h],
                )
            )
            copies[-1].start()
    for copy in copies:
        copy.wait()


def last(acc, near, lift, scale):
    return pl.pallas_call(
        last_kernel,
        out_shape=jax.ShapeDtypeStruct((STATE, EX, EY), F32),
        in_specs=[VMEM, VMEM, VMEM, VMEM],
        out_specs=ANY,
        scratch_shapes=[
            pltpu.VMEM((EX // 8, 2, STATE, 8, 128), F32),
            pltpu.SemaphoreType.DMA((EX // 8, 2)),
        ],
        compiler_params=pltpu.CompilerParams(vmem_limit_bytes=24 << 20),
        name="last",
    )(acc, near, lift, scale)


def local(
    adjoint_state, inverse_scale, element_inverse, trace_op, lift_op,
    obs_elem, obs_count, obs_basis, innovation,
):
    got = route(obs_elem, obs_count, obs_basis, innovation)
    acc, near, lift = steps(
        adjoint_state, inverse_scale, element_inverse, trace_op, lift_op, got
    )
    return last(acc, near, lift, inverse_scale)


def solution(mesh):
    placed = (
        P(None, "gx", "gy"),
        P("gx", "gy"),
        P(),
        P(),
        P(),
        P(None, ("gx", "gy")),
        P(None, ("gx", "gy")),
        P(None, None, ("gx", "gy")),
        P(None, ("gx", "gy")),
    )
    return jax.shard_map(
        local, mesh=mesh, in_specs=placed, out_specs=P(None, "gx", "gy"), check_vma=False
    )
```

profile of v0, /device:TPU:1, one launch (start us, length us, event | category | flops | bytes accessed | tf_op | source)
XLA Modules:
  0.0 82.8 jit_solution(16924760696240438491)
XLA Ops:
  0.0 0.7 copy.10.count_ref
  0.7 0.0 copy-start
  0.7 1.0 %copy-done = f32[2,64,768]{2,1,0:T(8,128)S(1)} copy-done((f32[2,64,768]{2,1,0:T(8,128)S(1)}, f32[2,64,768]{2,1,0:T(8,128)}, u32[]{:S(2)}) %copy-start) | copy-done | bytes 393240
  1.7 0.0 copy-start.5
  1.7 0.7 copy-done.5
  2.4 0.0 copy-start.6
  2.4 0.7 copy-done.6
  3.1 21.6 %route.1.got_ref = f32[1024,128]{1,0:T(8,128)S(1)} custom-call(s32[2,768]{1,0:T(2,128)S(1)} %copy-done.5, s32[2,1]{1,0:T(2,128)S(1)} %copy.10.count_ref, f32[2,64,768]{2,1,0:T(8,128)S(1)} %copy-done, f32[2,768]{1,0:T(2,128)S(1)} %copy-done.6), custom_call_target="tpu_custom_call" | custom-call | tf_op jit(solution)/shard_map/route/pallas_call | solution.py:129
  24.7 0.0 copy-start.1
  24.7 0.9 %copy-done.1 = f32[192,192]{1,0:T(8,128)S(1)} copy-done((f32[192,192]{1,0:T(8,128)S(1)}, f32[192,192]{1,0:T(8,128)}, u32[]{:S(2)}) %copy-start.1) | copy-done | bytes 147480
  25.6 0.0 copy-start.2
  25.6 0.8 copy-done.2
  26.4 0.0 copy-start.3
  26.4 0.9 %copy-done.3 = f32[96,192]{1,0:T(8,128)S(1)} copy-done((f32[96,192]{1,0:T(8,128)S(1)}, f32[96,192]{1,0:T(8,128)}, u32[]{:S(2)}) %copy-start.3) | copy-done | bytes 73752
  27.3 0.0 copy-start.4
  27.3 0.9 %copy-done.4 = f32[192,96]{1,0:T(8,128)S(1)} copy-done((f32[192,96]{1,0:T(8,128)S(1)}, f32[192,96]{1,0:T(8,128)}, u32[]{:S(2)}) %copy-start.4) | copy-done | bytes 73752
  28.2 45.6 %steps.1 = (f32[32,192,256]{2,1,0:T(8,128)S(1)}, f32[34,96,256]{2,1,0:T(8,128)S(1)}, bf16[2,192,96]{2,1,0:T(8,128)(2,1)S(1)}) custom-call(f32[192,32,256]{2,1,0:T(8,128)} %state_ref.1, f32[32,256]{1,0:T(8,128)S(1)} %copy-done.2, f32[192,192]{1,0:T(8,128)S(1)} %copy-done.1, f32[96,192]{1,0:T(8,128)S(1)} %copy-done.3, f32[192,96]{1,0:T(8,128)S(1)} %copy-done.4, ...), custom_call_target="tpu_custom_call" | custom-call | tf_op jit(solution)/shard_map/steps/pallas_call | solution.py:334
  73.8 9.0 %last.1 = f32[192,32,256]{2,1,0:T(8,128)} custom-call(f32[32,192,256]{2,1,0:T(8,128)S(1)} %get-tuple-element.8.acc_ref, f32[34,96,256]{2,1,0:T(8,128)S(1)} %get-tuple-element.9.near_ref, bf16[2,192,96]{2,1,0:T(8,128)(2,1)S(1)} %get-tuple-element.10.b_ref, f32[32,256]{1,0:T(8,128)S(1)} %copy-done.2), custom_call_target="tpu_custom_call" | custom-call | tf_op jit(solution)/shard_map/last/pallas_call | solution.py:394
Async XLA Ops:
  0.7 1.0 %copy-start = (f32[2,64,768]{2,1,0:T(8,128)S(1)}, f32[2,64,768]{2,1,0:T(8,128)}, u32[]{:S(2)}) copy-start(f32[2,64,768]{2,1,0:T(8,128)} %basis_ref.1) | copy-start | bytes 1179652
  1.7 0.7 copy-start.5
  2.4 0.7 copy-start.6
  24.7 0.9 %copy-start.1 = (f32[192,192]{1,0:T(8,128)S(1)}, f32[192,192]{1,0:T(8,128)}, u32[]{:S(2)}) copy-start(f32[192,192]{1,0:T(8,128)} %inverse_ref.1) | copy-start | bytes 442372
  25.6 0.8 copy-start.2
  26.4 0.9 %copy-start.3 = (f32[96,192]{1,0:T(8,128)S(1)}, f32[96,192]{1,0:T(8,128)}, u32[]{:S(2)}) copy-start(f32[96,192]{1,0:T(8,128)} %trace_ref.1) | copy-start | bytes 221188
  27.3 0.9 %copy-start.4 = (f32[192,96]{1,0:T(8,128)S(1)}, f32[192,96]{1,0:T(8,128)}, u32[]{:S(2)}) copy-start(f32[192,96]{1,0:T(8,128)} %lift_ref.1) | copy-start | bytes 221188
where the time goes:
time: 83.2 us; the launch traced here: 82.8 us
  Pallas kernels  76.2 us (92%)
  local copies, waits for them, and re-layouts  6.58 us (8%)
    pallas_call x1, Pallas kernels, steps(): pl.pallas_call(steps_kernel, out_shape=(pltpu.VMEM((EX, STATE, EY), F32),...  45.6 us
    pallas_call x1, Pallas kernels, route(): pl.pallas_call(route_kernel, out_shape=pltpu.VMEM((DEV * 8, 128), F32), i...  21.6 us
    pallas_call x1, Pallas kernels, last(): pl.pallas_call(last_kernel, out_shape=jax.ShapeDtypeStruct((STATE, EX, EY...  9.03 us
    unnamed x15, local copies, waits for them, and re-layouts  6.58 us

commit v1 on v0

v1 whole, which is shorter than its diff:
```python
import functools

import jax
import jax.numpy as jnp
from jax import lax
from jax.experimental import pallas as pl
from jax.experimental.pallas import tpu as pltpu
from jax.sharding import PartitionSpec as P

F32 = jnp.float32
BF = jnp.bfloat16
MESH = pl.DeviceIdType.MESH
STEPS = 2
NODES = 64
FN = 24
STATE = 192
EX = 32
EY = 256
OBS = 768
CAP = 6
GX = 8
GY = 16
DEV = GX * GY
VMEM = pl.BlockSpec(memory_space=pltpu.VMEM)
HBM = pl.BlockSpec(memory_space=pltpu.HBM)


def dot(a, b):
    return jnp.dot(a, b, preferred_element_type=F32)


def rows(*parts):
    return jnp.concatenate(parts, axis=0)


def lanes(*parts):
    return jnp.concatenate(parts, axis=1)


def dot_nt(a, b):
    return lax.dot_general(a, b, (((1,), (1,)), ((), ())), preferred_element_type=F32)


def dot_full(a, b):
    return jnp.dot(a, b, preferred_element_type=F32, precision=lax.Precision.HIGHEST)


def split(v):
    hi = v.astype(BF)
    return hi, (v - hi.astype(F32)).astype(BF)


def triple(v):
    hi, lo = split(v)
    return rows(hi, lo, hi)


def weights(v):
    hi, lo = split(v)
    hi, lo = hi.astype(F32), lo.astype(F32)
    return lanes(hi, hi, lo).astype(BF)


def tile(c, h):
    return pl.ds(pl.multiple_of((c * 2 + h) * STATE, 8), STATE)


def row(c, h, r):
    return pl.ds(pl.multiple_of((c * 2 + h) * STATE * 8, 8) + r, STATE, stride=8)


def iota(shape, dim):
    return lax.broadcasted_iota(jnp.int32, shape, dim)


def pack(elem_ref, count_ref, basis_ref, innov_ref, out_ref):
    lane = iota((1, OBS), 1)
    owner = iota((DEV, OBS), 0)
    tri = (iota((256, 256), 0) < iota((256, 256), 1)).astype(F32).astype(BF)
    row = iota((128, OBS), 0)
    halves = []
    ids = jnp.zeros((DEV, 128), F32)
    for s in range(STEPS):
        elem = elem_ref[s : s + 1, :]
        gx = lax.shift_right_logical(elem, 17)
        lx = lax.shift_right_logical(elem, 12) & (EX - 1)
        gy = lax.shift_right_logical(elem, 8) & (GY - 1)
        ly = elem & (EY - 1)
        live = lane < count_ref[0:1, s : s + 1]
        target = jnp.where(live, gx * GY + gy, -1)
        member = (owner == target).astype(F32)
        carry = jnp.zeros((DEV, 1), F32)
        running = []
        for b in range(OBS // 256):
            part = member[:, b * 256 : (b + 1) * 256]
            running.append(dot(part.astype(BF), tri) + carry)
            carry = carry + jnp.sum(part, axis=1, keepdims=True)
        before = jnp.concatenate(running, axis=1)
        rank = jnp.sum(member * before, axis=0, keepdims=True).astype(jnp.int32)
        hi, lo = split(basis_ref[s] * innov_ref[s : s + 1, :])
        both = jnp.concatenate([hi, lo], axis=0)
        picked = []
        for j in range(CAP):
            chosen = jnp.where(rank == j, member, 0.0).astype(BF)
            got = dot_nt(chosen, both)
            picked.append(got + pltpu.roll(got, 64, 1))
        halves.append(picked)
        where = jnp.where(row == rank + 16 * s, lx + 1, 0)
        where = where + jnp.where(row == rank + 16 * s + 8, ly, 0)
        ids = ids + dot_nt(member.astype(BF), where.astype(F32).astype(BF))
    low = iota((DEV, 128), 1) < 64
    for j in range(CAP):
        out_ref[pl.ds(j, DEV, stride=8), :] = jnp.where(low, halves[0][j], halves[1][j])
    out_ref[pl.ds(CAP, DEV, stride=8), :] = ids
    out_ref[pl.ds(CAP + 1, DEV, stride=8), :] = jnp.zeros((DEV, 128), F32)


def unpack(got_ref, pay_ref, col_ref, rowid_ref):
    ids = got_ref[pl.ds(CAP, DEV, stride=8), :].T
    parts = [got_ref[pl.ds(j, DEV, stride=8), :].T for j in range(CAP)]
    for s in range(STEPS):
        values = jnp.concatenate([p[s * 64 : s * 64 + 64] for p in parts], axis=1)
        hi, lo = split(values)
        pay_ref[s, :, 0:OBS] = hi
        pay_ref[s, :, OBS : 2 * OBS] = lo
        xs = [ids[s * 16 + j : s * 16 + j + 1, :] for j in range(CAP)]
        ys = [ids[s * 16 + 8 + j : s * 16 + 9 + j, :] for j in range(CAP)]
        rowid_ref[s : s + 1, :] = jnp.concatenate(xs, axis=1).astype(jnp.int32) - 1
        ycol = jnp.concatenate(ys, axis=1).astype(jnp.int32)
        hot = (iota((EY, OBS), 0) == ycol).astype(F32)
        hot = hot.T.astype(BF)
        col_ref[s, 0:OBS, :] = hot
        col_ref[s, OBS : 2 * OBS, :] = hot


def force(s, pay_ref, col_ref, rowid_ref, force_ref):
    group = 16

    def body(g, carry):
        rowid = rowid_ref[s : s + 1, :]
        pay = pay_ref[s]
        stack = []
        for i in range(group):
            here = (rowid == g * group + i).astype(F32).astype(BF)
            stack.append(pay * lanes(here, here))
        got = dot(rows(*stack), col_ref[s])
        for i in range(group):
            force_ref[s, g * group + i] = got[i * NODES : i * NODES + NODES]
        return carry

    lax.fori_loop(0, EX // group, body, 0)


def put(x, tr, near_ref, carry):
    down, up = carry
    near_ref[x, FN : 2 * FN, :] = tr[0:FN]
    near_ref[x + 2, 0:FN, :] = tr[FN : 2 * FN]
    from_south = pltpu.roll(tr[3 * FN : 4 * FN], 1, 1)
    from_north = pltpu.roll(tr[2 * FN : 3 * FN], EY - 1, 1)
    near_ref[x + 1, 2 * FN : 3 * FN, :] = from_south
    near_ref[x + 1, 3 * FN : 4 * FN, :] = from_north
    here = iota((FN, 128), 1) == x
    up = jnp.where(here, from_south[:, 0:1], up)
    down = jnp.where(here, from_north[:, EY - 1 : EY], down)
    return down, up


def patch(near_ref, below, above):
    first = iota((FN, 128), 1) == 0
    last = iota((FN, 128), 1) == 127
    south, north = slice(2 * FN, 3 * FN), slice(3 * FN, 4 * FN)

    def body(x, carry):
        low = pltpu.roll(below, (128 - x) % 128, 1)
        high = pltpu.roll(above, 127 - x, 1)
        near_ref[x + 1, south, 0:128] = jnp.where(first, low, near_ref[x + 1, south, 0:128])
        near_ref[x + 1, north, 128:256] = jnp.where(last, high, near_ref[x + 1, north, 128:256])
        return carry

    lax.fori_loop(0, EX, body, 0, unroll=8)


def finish(x, acc_ref, near_ref, b_ref, scale_ref):
    lifted = dot(b_ref[...], triple(near_ref[x + 1]))
    return (acc_ref[x] + lifted) * scale_ref[pl.ds(x, 1), :]


def main_kernel(
    state_hbm, scale_hbm, inverse_hbm, trace_hbm, lift_hbm, elem_hbm, count_hbm, basis_hbm, innov_hbm,
    acc_ref, near2_ref, b_ref, scale_ref,
    stage, slab, near1_ref, tr_ref, force_ref, pay_ref, col_ref, rowid_ref, at_ref, c_ref,
    inverse_ref, trace_ref, lift_ref, elem_ref, count_ref, basis_ref, innov_ref,
    out_ref, got_ref, ysend, yrecv,
    load_sem, small_sem, far_sem, near_send, near_recv, all_in,
):
    px, py = lax.axis_index("gx"), lax.axis_index("gy")
    me = px * GY + py
    small = []
    for k, (src, dst) in enumerate(
        (
            (elem_hbm, elem_ref), (count_hbm, count_ref), (basis_hbm, basis_ref),
            (innov_hbm, innov_ref), (inverse_hbm, inverse_ref), (trace_hbm, trace_ref),
            (lift_hbm, lift_ref), (scale_hbm, scale_ref),
        )
    ):
        small.append(pltpu.make_async_copy(src, dst, small_sem.at[k]))
        small[-1].start()

    def load(c, h):
        column = slice(h * 128, h * 128 + 128)
        band = pl.ds(pl.multiple_of(c * 8, 8), 8)
        return pltpu.make_async_copy(
            state_hbm.at[:, band, column], stage.at[tile(c, h)], load_sem.at[c, h]
        )

    for c in range(EX // 8):
        for h in range(2):
            load(c, h).start()
    barrier = pltpu.get_barrier_semaphore()

    row_peers = [((px + k) % GX, py) for k in range(1, GX)]
    column_peers = [(px, (py + k) % GY) for k in range(1, GY)]
    for peer in row_peers + column_peers:
        pl.semaphore_signal(barrier, inc=1, device_id=peer, device_id_type=MESH)
    for copy in small:
        copy.wait()
    operator = trace_ref[...]
    inverse = inverse_ref[...]
    half = 0.5 * dot_full(inverse, lift_ref[...])
    whole = inverse + dot_full(half, operator)
    at_ref[...] = weights(rows(whole, operator))
    c_ref[...] = weights(rows(whole, operator)[:, 0:NODES])
    b_ref[...] = weights(half)
    pl.semaphore_wait(barrier, GX + GY - 2)
    for peer in column_peers:
        pl.semaphore_signal(all_in, inc=1, device_id=peer, device_id_type=MESH)
    pack(elem_ref, count_ref, basis_ref, innov_ref, out_ref)
    mine = pl.ds(pl.multiple_of(me * 8, 8), 8)
    got_ref[mine, :] = out_ref[mine, :]
    pl.semaphore_wait(all_in, GY - 1)

    def send(k):
        peer = (me + k) % DEV
        pltpu.make_async_remote_copy(
            src_ref=out_ref.at[pl.ds(pl.multiple_of(peer * 8, 8), 8)],
            dst_ref=got_ref.at[mine],
            send_sem=far_sem.at[0],
            recv_sem=far_sem.at[1],
            device_id=(peer // GY, peer % GY),
            device_id_type=MESH,
        ).start()

    flat = stage.reshape(EX // 4 * STATE * 8, 128)

    def begin(c, carry):
        for h in range(2):
            load(c, h).wait()
        for r in range(8):
            if r % 4 == 0:
                for u in range(4 * 4):
                    k = c * 32 + r * 4 + u + 1
                    if r * 4 + u == 31:
                        pl.when(k < DEV)(functools.partial(send, k))
                    else:
                        send(k)
            x = c * 8 + r
            halves = [flat[row(c, h, r), :] for h in range(2)]
            both = dot(at_ref[...], triple(lanes(*halves)))
            acc_ref[x] = both[0:STATE]
            tr_ref[x] = both[STATE:]
        return carry

    lax.fori_loop(0, EX // 8, begin, 0)
    rest = pl.ds(0, (DEV - 1) * 8)
    pltpu.make_async_copy(out_ref.at[rest], out_ref.at[rest], far_sem.at[0]).wait()
    pltpu.make_async_copy(got_ref.at[rest], got_ref.at[rest], far_sem.at[1]).wait()
    unpack(got_ref, pay_ref, col_ref, rowid_ref)
    force(0, pay_ref, col_ref, rowid_ref, force_ref)

    peers = (
        (lax.rem(px + GX - 1, GX), py),
        (lax.rem(px + 1, GX), py),
        (px, lax.rem(py + GY - 1, GY)),
        (px, lax.rem(py + 1, GY)),
    )

    def send_halos(s, near_ref, down, up):
        ysend[s, 0] = down
        ysend[s, 1] = up
        pairs = (
            (near_ref.at[0, FN : 2 * FN], near_ref.at[EX, FN : 2 * FN]),
            (near_ref.at[EX + 1, 0:FN], near_ref.at[1, 0:FN]),
            (ysend.at[s, 0], yrecv.at[s, 1]),
            (ysend.at[s, 1], yrecv.at[s, 0]),
        )
        copies = []
        for k in range(4):
            copies.append(
                pltpu.make_async_remote_copy(
                    src_ref=pairs[k][0],
                    dst_ref=pairs[k][1],
                    send_sem=near_send.at[s, k],
                    recv_sem=near_recv.at[s, k],
                    device_id=peers[k],
                    device_id_type=MESH,
                )
            )
            copies[-1].start()
        return copies

    def take_halos(s, near_ref, copies):
        for copy in copies:
            copy.wait()
        below = jnp.where(py == 0, ysend[s, 0], yrecv[s, 0])
        above = jnp.where(py == GY - 1, ysend[s, 1], yrecv[s, 1])
        patch(near_ref, below, above)

    def correct(x, carry):
        both = dot(c_ref[...], triple(force_ref[0, x]))
        acc_ref[x] += both[0:STATE]
        return put(x, tr_ref[x] + both[STATE:], near1_ref, carry)

    def middle(x, carry):
        value = finish(x, acc_ref, near1_ref, b_ref, scale_ref)
        hi, lo = split(rows(value[0:NODES] + force_ref[1, x], value[NODES:STATE]))
        slab[x, 0:STATE, :] = hi
        slab[x, STATE : 2 * STATE, :] = lo
        return carry

    def trace(x, carry):
        tr = dot(at_ref[STATE : STATE + 4 * FN, :], rows(slab[x], slab[x, 0:STATE, :]))
        return put(x, tr, near2_ref, carry)

    def hold(x, carry):
        acc_ref[x] = dot(at_ref[0:STATE, :], rows(slab[x], slab[x, 0:STATE, :]))
        return carry

    rim = jnp.zeros((FN, 128), F32)
    down, up = lax.fori_loop(0, EX, correct, (rim, rim), unroll=8)
    copies = send_halos(0, near1_ref, down, up)
    force(1, pay_ref, col_ref, rowid_ref, force_ref)
    take_halos(0, near1_ref, copies)
    lax.fori_loop(0, EX, middle, 0, unroll=8)
    down, up = lax.fori_loop(0, EX, trace, (rim, rim), unroll=8)
    copies = send_halos(1, near2_ref, down, up)
    lax.fori_loop(0, EX, hold, 0, unroll=8)
    take_halos(1, near2_ref, copies)


def last_kernel(acc_ref, near_ref, b_ref, scale_ref, out_ref, stage, sem):
    def store(c, h):
        band = pl.ds(pl.multiple_of(c * 8, 8), 8)
        column = slice(h * 128, h * 128 + 128)
        return pltpu.make_async_copy(
            stage.at[tile(c, h)], out_ref.at[:, band, column], sem.at[c, h]
        )

    flat = stage.reshape(EX // 4 * STATE * 8, 128)

    def body(c, carry):
        for r in range(8):
            value = finish(c * 8 + r, acc_ref, near_ref, b_ref, scale_ref)
            for h in range(2):
                flat[row(c, h, r), :] = value[:, h * 128 : h * 128 + 128]
        for h in range(2):
            store(c, h).start()
        return carry

    lax.fori_loop(0, EX // 8, body, 0)
    for c in range(EX // 8):
        for h in range(2):
            store(c, h).wait()


def local(
    adjoint_state, inverse_scale, element_inverse, trace_op, lift_op,
    obs_elem, obs_count, obs_basis, innovation,
):
    acc, near, lift, scale = pl.pallas_call(
        main_kernel,
        out_shape=(
            pltpu.VMEM((EX, STATE, EY), F32),
            pltpu.VMEM((EX + 2, 4 * FN, EY), F32),
            pltpu.VMEM((STATE, 12 * FN), BF),
            pltpu.VMEM((EX, EY), F32),
        ),
        in_specs=[HBM] * 9,
        out_specs=(VMEM, VMEM, VMEM, VMEM),
        scratch_shapes=[
            pltpu.VMEM((EX // 4 * STATE, 8, 128), F32),
            pltpu.VMEM((EX, 2 * STATE, EY), BF),
            pltpu.VMEM((EX + 2, 4 * FN, EY), F32),
            pltpu.VMEM((EX, 4 * FN, EY), F32),
            pltpu.VMEM((STEPS, EX, NODES, EY), F32),
            pltpu.VMEM((STEPS, NODES, 2 * OBS), BF),
            pltpu.VMEM((STEPS, 2 * OBS, EY), BF),
            pltpu.VMEM((8, OBS), jnp.int32),
            pltpu.VMEM((STATE + 4 * FN, 3 * STATE), BF),
            pltpu.VMEM((STATE + 4 * FN, 3 * NODES), BF),
            pltpu.VMEM((STATE, STATE), F32),
            pltpu.VMEM((4 * FN, STATE), F32),
            pltpu.VMEM((STATE, 4 * FN), F32),
            pltpu.VMEM((STEPS, OBS), jnp.int32),
            pltpu.VMEM((1, STEPS), jnp.int32),
            pltpu.VMEM((STEPS, NODES, OBS), F32),
            pltpu.VMEM((STEPS, OBS), F32),
            pltpu.VMEM((DEV * 8, 128), F32),
            pltpu.VMEM((DEV * 8, 128), F32),
            pltpu.VMEM((STEPS, 2, FN, 128), F32),
            pltpu.VMEM((STEPS, 2, FN, 128), F32),
            pltpu.SemaphoreType.DMA((EX // 8, 2)),
            pltpu.SemaphoreType.DMA((8,)),
            pltpu.SemaphoreType.DMA((2,)),
            pltpu.SemaphoreType.DMA((STEPS, 4)),
            pltpu.SemaphoreType.DMA((STEPS, 4)),
            pltpu.SemaphoreType.REGULAR,
        ],
        compiler_params=pltpu.CompilerParams(
            collective_id=0, has_side_effects=True, vmem_limit_bytes=40 << 20
        ),
        name="main",
    )(
        *(
            pltpu.with_memory_space_constraint(v, pltpu.HBM)
            for v in (
                adjoint_state, inverse_scale, element_inverse, trace_op, lift_op,
                obs_elem, obs_count.T, obs_basis, innovation,
            )
        )
    )
    return pl.pallas_call(
        last_kernel,
        out_shape=jax.ShapeDtypeStruct((STATE, EX, EY), F32),
        in_specs=[VMEM, VMEM, VMEM, VMEM],
        out_specs=HBM,
        scratch_shapes=[
            pltpu.VMEM((EX // 4 * STATE, 8, 128), F32),
            pltpu.SemaphoreType.DMA((EX // 8, 2)),
        ],
        compiler_params=pltpu.CompilerParams(vmem_limit_bytes=24 << 20),
        name="last",
    )(acc, near, lift, scale)


def solution(mesh):
    placed = (
        P(None, "gx", "gy"),
        P("gx", "gy"),
        P(),
        P(),
        P(),
        P(None, ("gx", "gy")),
        P(None, ("gx", "gy")),
        P(None, None, ("gx", "gy")),
        P(None, ("gx", "gy")),
    )
    return jax.shard_map(
        local, mesh=mesh, in_specs=placed, out_specs=P(None, "gx", "gy"), check_vma=False
    )
```

time: 83.2 us -> 47.3 us (0.57)
  Pallas kernels: 76.2 us -> 47.2 us
  local copies, waits for them, and re-layouts: 6.58 us -> 0 us
    pallas_call x3 -> x2, Pallas kernels: 76.2 us -> 47.2 us  [the longest x1 43.4 us: local(): pl.pallas_call(main_kernel, out_shape=(pltpu.VMEM((EX, STATE, EY), F32),...]
    unnamed x15 -> x0, local copies, waits for them, and re-layouts: 6.58 us -> none
where the time goes in v1:
time: 47.3 us; the launch traced here: 47.2 us
  Pallas kernels  47.2 us (100%)
    pallas_call x1, Pallas kernels, local(): pl.pallas_call(main_kernel, out_shape=(pltpu.VMEM((EX, STATE, EY), F32),...  43.4 us
    pallas_call x1, Pallas kernels, local(): pl.pallas_call(last_kernel, out_shape=jax.ShapeDtypeStruct((STATE, EX, EY...  3.74 us

profile of v1, /device:TPU:1, one launch (start us, length us, event | category | flops | bytes accessed | tf_op | source)
XLA Modules:
  0.0 47.2 jit_solution(7458660394369851630)
XLA Ops:
  0.0 43.4 %main.1 = (f32[32,192,256]{2,1,0:T(8,128)S(1)}, f32[34,96,256]{2,1,0:T(8,128)S(1)}, bf16[192,288]{1,0:T(8,128)(2,1)S(1)}, f32[32,256]{1,0:T(8,128)S(1)}) custom-call(f32[192,32,256]{2,1,0:T(8,128)} %state_hbm.1, f32[32,256]{1,0:T(8,128)} %scale_hbm.1, f32[192,192]{1,0:T(8,128)} %inverse_hbm.1, f32[96,192]{1,0:T(8,128)} %trace_hbm.1, f32[192,96]{1,0:T(8,128)} %lift_hbm.1, ...), custom_call_target="tpu_custom_call" | custom-call | tf_op jit(solution)/shard_map/main/pallas_call | solution.py:379
  43.4 3.7 %last.1 = f32[192,32,256]{2,1,0:T(8,128)} custom-call(f32[32,192,256]{2,1,0:T(8,128)S(1)} %get-tuple-element.9.acc_ref, f32[34,96,256]{2,1,0:T(8,128)S(1)} %get-tuple-element.10.near_ref, bf16[192,288]{1,0:T(8,128)(2,1)S(1)} %get-tuple-element.11.b_ref, f32[32,256]{1,0:T(8,128)S(1)} %get-tuple-element.12.scale_ref), custom_call_target="tpu_custom_call" | custom-call | tf_op jit(solution)/shard_map/last/pallas_call | solution.py:431

commit v2 on v1

--- a/solution.py
+++ b/solution.py
@@ -18,6 +18,7 @@
 EY = 256
 OBS = 768
 CAP = 6
+USED = CAP + 1
 GX = 8
 GY = 16
 DEV = GX * GY
@@ -112,7 +113,6 @@
     for j in range(CAP):
         out_ref[pl.ds(j, DEV, stride=8), :] = jnp.where(low, halves[0][j], halves[1][j])
     out_ref[pl.ds(CAP, DEV, stride=8), :] = ids
-    out_ref[pl.ds(CAP + 1, DEV, stride=8), :] = jnp.zeros((DEV, 128), F32)
 
 
 def unpack(got_ref, pay_ref, col_ref, rowid_ref):
@@ -222,7 +222,29 @@
     column_peers = [(px, (py + k) % GY) for k in range(1, GY)]
     for peer in row_peers + column_peers:
         pl.semaphore_signal(barrier, inc=1, device_id=peer, device_id_type=MESH)
-    for copy in small:
+    for copy in small[0:4]:
+        copy.wait()
+    pack(elem_ref, count_ref, basis_ref, innov_ref, out_ref)
+    mine = pl.ds(pl.multiple_of(me * 8, 8), USED)
+    got_ref[mine, :] = out_ref[mine, :]
+    pl.semaphore_wait(barrier, GX + GY - 2)
+    for peer in column_peers:
+        pl.semaphore_signal(all_in, inc=1, device_id=peer, device_id_type=MESH)
+
+    def send(peer):
+        to = peer[0] * GY + peer[1]
+        pltpu.make_async_remote_copy(
+            src_ref=out_ref.at[pl.ds(pl.multiple_of(to * 8, 8), USED)],
+            dst_ref=got_ref.at[mine],
+            send_sem=far_sem.at[0],
+            recv_sem=far_sem.at[1],
+            device_id=peer,
+            device_id_type=MESH,
+        ).start()
+
+    for peer in row_peers + column_peers:
+        send(peer)
+    for copy in small[4:]:
         copy.wait()
     operator = trace_ref[...]
     inverse = inverse_ref[...]
@@ -231,47 +253,33 @@
     at_ref[...] = weights(rows(whole, operator))
     c_ref[...] = weights(rows(whole, operator)[:, 0:NODES])
     b_ref[...] = weights(half)
-    pl.semaphore_wait(barrier, GX + GY - 2)
-    for peer in column_peers:
-        pl.semaphore_signal(all_in, inc=1, device_id=peer, device_id_type=MESH)
-    pack(elem_ref, count_ref, basis_ref, innov_ref, out_ref)
-    mine = pl.ds(pl.multiple_of(me * 8, 8), 8)
-    got_ref[mine, :] = out_ref[mine, :]
-    pl.semaphore_wait(all_in, GY - 1)
-
-    def send(k):
-        peer = (me + k) % DEV
-        pltpu.make_async_remote_copy(
-            src_ref=out_ref.at[pl.ds(pl.multiple_of(peer * 8, 8), 8)],
-            dst_ref=got_ref.at[mine],
-            send_sem=far_sem.at[0],
-            recv_sem=far_sem.at[1],
-            device_id=(peer // GY, peer % GY),
-            device_id_type=MESH,
-        ).start()
 
     flat = stage.reshape(EX // 4 * STATE * 8, 128)
 
-    def begin(c, carry):
+    def begin(c):
         for h in range(2):
             load(c, h).wait()
         for r in range(8):
-            if r % 4 == 0:
-                for u in range(4 * 4):
-                    k = c * 32 + r * 4 + u + 1
-                    if r * 4 + u == 31:
-                        pl.when(k < DEV)(functools.partial(send, k))
-                    else:
-                        send(k)
             x = c * 8 + r
             halves = [flat[row(c, h, r), :] for h in range(2)]
             both = dot(at_ref[...], triple(lanes(*halves)))
             acc_ref[x] = both[0:STATE]
             tr_ref[x] = both[STATE:]
-        return carry
-
-    lax.fori_loop(0, EX // 8, begin, 0)
-    rest = pl.ds(0, (DEV - 1) * 8)
+
+    far = (GX - 1) * (GY - 1)
+    share = far // (EX // 8 - 1)
+
+    def begin_and_send(c, carry):
+        for u in range(share):
+            k = ((c - 1) * share + u) * 52 % far
+            send(((px + 1 + k // (GY - 1)) % GX, (py + 1 + k % (GY - 1)) % GY))
+        begin(c)
+        return carry
+
+    begin(0)
+    pl.semaphore_wait(all_in, GY - 1)
+    lax.fori_loop(1, EX // 8, begin_and_send, 0)
+    rest = pl.ds(0, (DEV - 1) * USED)
     pltpu.make_async_copy(out_ref.at[rest], out_ref.at[rest], far_sem.at[0]).wait()
     pltpu.make_async_copy(got_ref.at[rest], got_ref.at[rest], far_sem.at[1]).wait()
     unpack(got_ref, pay_ref, col_ref, rowid_ref)
@@ -315,10 +323,13 @@
         above = jnp.where(py == GY - 1, ysend[s, 1], yrecv[s, 1])
         patch(near_ref, below, above)
 
+    def correct_traces(x, carry):
+        tr = dot(c_ref[STATE : STATE + 4 * FN, :], triple(force_ref[0, x]))
+        return put(x, tr_ref[x] + tr, near1_ref, carry)
+
     def correct(x, carry):
-        both = dot(c_ref[...], triple(force_ref[0, x]))
-        acc_ref[x] += both[0:STATE]
-        return put(x, tr_ref[x] + both[STATE:], near1_ref, carry)
+        acc_ref[x] += dot(c_ref[0:STATE, :], triple(force_ref[0, x]))
+        return carry
 
     def middle(x, carry):
         value = finish(x, acc_ref, near1_ref, b_ref, scale_ref)
@@ -336,14 +347,15 @@
         return carry
 
     rim = jnp.zeros((FN, 128), F32)
-    down, up = lax.fori_loop(0, EX, correct, (rim, rim), unroll=8)
+    down, up = lax.fori_loop(0, EX, correct_traces, (rim, rim), unroll=16)
     copies = send_halos(0, near1_ref, down, up)
+    lax.fori_loop(0, EX, correct, 0, unroll=16)
     force(1, pay_ref, col_ref, rowid_ref, force_ref)
     take_halos(0, near1_ref, copies)
-    lax.fori_loop(0, EX, middle, 0, unroll=8)
-    down, up = lax.fori_loop(0, EX, trace, (rim, rim), unroll=8)
+    lax.fori_loop(0, EX, middle, 0, unroll=16)
+    down, up = lax.fori_loop(0, EX, trace, (rim, rim), unroll=16)
     copies = send_halos(1, near2_ref, down, up)
-    lax.fori_loop(0, EX, hold, 0, unroll=8)
+    lax.fori_loop(0, EX, hold, 0, unroll=16)
     take_halos(1, near2_ref, copies)
 
 

time: 47.3 us -> 42.6 us (0.901)
  Pallas kernels: 47.2 us -> 42.3 us
    pallas_call x1, Pallas kernels: 43.4 us -> 38.5 us  [local(): pl.pallas_call(main_kernel, out_shape=(pltpu.VMEM((EX, STATE, EY), F32),...]
where the time goes in v2:
time: 42.6 us; the launch traced here: 42.4 us
  Pallas kernels  42.3 us (99%)
    pallas_call x1, Pallas kernels, local(): pl.pallas_call(main_kernel, out_shape=(pltpu.VMEM((EX, STATE, EY), F32),...  38.5 us
    pallas_call x1, Pallas kernels, local(): pl.pallas_call(last_kernel, out_shape=jax.ShapeDtypeStruct((STATE, EX, EY...  3.74 us

profile of v2, /device:TPU:1, one launch (start us, length us, event | category | flops | bytes accessed | tf_op | source)
XLA Modules:
  0.0 42.4 jit_solution(3627920268234572235)
XLA Ops:
  0.0 38.5 %main.1 = (f32[32,192,256]{2,1,0:T(8,128)S(1)}, f32[34,96,256]{2,1,0:T(8,128)S(1)}, bf16[192,288]{1,0:T(8,128)(2,1)S(1)}, f32[32,256]{1,0:T(8,128)S(1)}) custom-call(f32[192,32,256]{2,1,0:T(8,128)} %state_hbm.1, f32[32,256]{1,0:T(8,128)} %scale_hbm.1, f32[192,192]{1,0:T(8,128)} %inverse_hbm.1, f32[96,192]{1,0:T(8,128)} %trace_hbm.1, f32[192,96]{1,0:T(8,128)} %lift_hbm.1, ...), custom_call_target="tpu_custom_call" | custom-call | tf_op jit(solution)/shard_map/main/pallas_call | solution.py:391
  38.5 3.7 %last.1 = f32[192,32,256]{2,1,0:T(8,128)} custom-call(f32[32,192,256]{2,1,0:T(8,128)S(1)} %get-tuple-element.9.acc_ref, f32[34,96,256]{2,1,0:T(8,128)S(1)} %get-tuple-element.10.near_ref, bf16[192,288]{1,0:T(8,128)(2,1)S(1)} %get-tuple-element.11.b_ref, f32[32,256]{1,0:T(8,128)S(1)} %get-tuple-element.12.scale_ref), custom_call_target="tpu_custom_call" | custom-call | tf_op jit(solution)/shard_map/last/pallas_call | solution.py:443

commit v3 on v2

--- a/solution.py
+++ b/solution.py
@@ -22,6 +22,8 @@
 GX = 8
 GY = 16
 DEV = GX * GY
+PART = DEV // 2
+HOT = PART * CAP
 VMEM = pl.BlockSpec(memory_space=pltpu.VMEM)
 HBM = pl.BlockSpec(memory_space=pltpu.HBM)
 
@@ -115,37 +117,47 @@
     out_ref[pl.ds(CAP, DEV, stride=8), :] = ids
 
 
-def unpack(got_ref, pay_ref, col_ref, rowid_ref):
-    ids = got_ref[pl.ds(CAP, DEV, stride=8), :].T
-    parts = [got_ref[pl.ds(j, DEV, stride=8), :].T for j in range(CAP)]
+def unpack(part, got_ref, pay_ref, col_ref, rowid_ref):
+    def get(j):
+        return got_ref[pl.ds(part * PART * 8 + j, PART, stride=8), :]
+
+    low = iota((1, 128), 1) < PART
+    ids = rows(get(CAP), get(CAP)).T
+    values = [rows(get(j), get(j + 1)).T for j in range(0, CAP, 2)]
     for s in range(STEPS):
-        values = jnp.concatenate([p[s * 64 : s * 64 + 64] for p in parts], axis=1)
-        hi, lo = split(values)
-        pay_ref[s, :, 0:OBS] = hi
-        pay_ref[s, :, OBS : 2 * OBS] = lo
-        xs = [ids[s * 16 + j : s * 16 + j + 1, :] for j in range(CAP)]
-        ys = [ids[s * 16 + 8 + j : s * 16 + 9 + j, :] for j in range(CAP)]
-        rowid_ref[s : s + 1, :] = jnp.concatenate(xs, axis=1).astype(jnp.int32) - 1
-        ycol = jnp.concatenate(ys, axis=1).astype(jnp.int32)
-        hot = (iota((EY, OBS), 0) == ycol).astype(F32)
-        hot = hot.T.astype(BF)
-        col_ref[s, 0:OBS, :] = hot
-        col_ref[s, OBS : 2 * OBS, :] = hot
-
-
-def force(s, pay_ref, col_ref, rowid_ref, force_ref):
+        hi, lo = split(lanes(*[v[s * NODES : s * NODES + NODES] for v in values]))
+        pay_ref[s, :, 2 * HOT * part : 2 * HOT * part + HOT] = hi
+        pay_ref[s, :, 2 * HOT * part + HOT : 2 * HOT * (part + 1)] = lo
+
+        def spread(first):
+            at = [ids[first + j : first + j + 1, :] for j in range(CAP)]
+            at = [jnp.where(low, at[j], at[j + 1]) for j in range(0, CAP, 2)]
+            return lanes(*at).astype(jnp.int32)
+
+        rowid_ref[s : s + 1, HOT * part : HOT * part + HOT] = spread(s * 16) - 1
+        hot = (iota((EY, HOT), 0) == spread(s * 16 + 8)).astype(F32).T.astype(BF)
+        col_ref[s, 2 * HOT * part : 2 * HOT * part + HOT, :] = hot
+        col_ref[s, 2 * HOT * part + HOT : 2 * HOT * (part + 1), :] = hot
+
+
+def force(s, parts, pay_ref, col_ref, rowid_ref, force_ref):
     group = 16
+    start, stop = parts[0], parts[-1] + 1
 
     def body(g, carry):
-        rowid = rowid_ref[s : s + 1, :]
-        pay = pay_ref[s]
+        rowid = rowid_ref[s : s + 1, HOT * start : HOT * stop]
+        pay = pay_ref[s, :, 2 * HOT * start : 2 * HOT * stop]
         stack = []
         for i in range(group):
             here = (rowid == g * group + i).astype(F32).astype(BF)
-            stack.append(pay * lanes(here, here))
-        got = dot(rows(*stack), col_ref[s])
+            here = [here[:, HOT * p : HOT * p + HOT] for p in range(stop - start)]
+            stack.append(pay * lanes(*[here[p // 2] for p in range(2 * len(here))]))
+        got = dot(rows(*stack), col_ref[s, 2 * HOT * start : 2 * HOT * stop, :])
         for i in range(group):
-            force_ref[s, g * group + i] = got[i * NODES : i * NODES + NODES]
+            mine = got[i * NODES : i * NODES + NODES]
+            if start > 0:
+                mine = mine + force_ref[s, g * group + i]
+            force_ref[s, g * group + i] = mine
         return carry
 
     lax.fori_loop(0, EX // group, body, 0)
@@ -165,29 +177,21 @@
     return down, up
 
 
-def patch(near_ref, below, above):
-    first = iota((FN, 128), 1) == 0
-    last = iota((FN, 128), 1) == 127
-    south, north = slice(2 * FN, 3 * FN), slice(3 * FN, 4 * FN)
-
-    def body(x, carry):
-        low = pltpu.roll(below, (128 - x) % 128, 1)
-        high = pltpu.roll(above, 127 - x, 1)
-        near_ref[x + 1, south, 0:128] = jnp.where(first, low, near_ref[x + 1, south, 0:128])
-        near_ref[x + 1, north, 128:256] = jnp.where(last, high, near_ref[x + 1, north, 128:256])
-        return carry
-
-    lax.fori_loop(0, EX, body, 0, unroll=8)
-
-
-def finish(x, acc_ref, near_ref, b_ref, scale_ref):
-    lifted = dot(b_ref[...], triple(near_ref[x + 1]))
+def finish(x, acc_ref, near_ref, rim_ref, b_ref, scale_ref):
+    lane = iota((FN, 128), 1)
+    below = pltpu.roll(rim_ref[0], (128 - x) % 128, 1)
+    above = pltpu.roll(rim_ref[1], 127 - x, 1)
+    near = near_ref[x + 1]
+    south, north = near[2 * FN : 3 * FN], near[3 * FN : 4 * FN]
+    south = lanes(jnp.where(lane == 0, below, south[:, 0:128]), south[:, 128:256])
+    north = lanes(north[:, 0:128], jnp.where(lane == 127, above, north[:, 128:256]))
+    lifted = dot(b_ref[...], triple(rows(near[0 : 2 * FN], south, north)))
     return (acc_ref[x] + lifted) * scale_ref[pl.ds(x, 1), :]
 
 
 def main_kernel(
     state_hbm, scale_hbm, inverse_hbm, trace_hbm, lift_hbm, elem_hbm, count_hbm, basis_hbm, innov_hbm,
-    acc_ref, near2_ref, b_ref, scale_ref,
+    acc_ref, near2_ref, rim_ref, b_ref, scale_ref,
     stage, slab, near1_ref, tr_ref, force_ref, pay_ref, col_ref, rowid_ref, at_ref, c_ref,
     inverse_ref, trace_ref, lift_ref, elem_ref, count_ref, basis_ref, innov_ref,
     out_ref, got_ref, ysend, yrecv,
@@ -195,6 +199,11 @@
 ):
     px, py = lax.axis_index("gx"), lax.axis_index("gy")
     me = px * GY + py
+    barrier = pltpu.get_barrier_semaphore()
+    row_peers = [((px + k) % GX, py) for k in range(1, GX)]
+    column_peers = [(px, (py + k) % GY) for k in range(1, GY)]
+    for peer in row_peers + column_peers:
+        pl.semaphore_signal(barrier, inc=1, device_id=peer, device_id_type=MESH)
     small = []
     for k, (src, dst) in enumerate(
         (
@@ -216,34 +225,28 @@
     for c in range(EX // 8):
         for h in range(2):
             load(c, h).start()
-    barrier = pltpu.get_barrier_semaphore()
-
-    row_peers = [((px + k) % GX, py) for k in range(1, GX)]
-    column_peers = [(px, (py + k) % GY) for k in range(1, GY)]
-    for peer in row_peers + column_peers:
-        pl.semaphore_signal(barrier, inc=1, device_id=peer, device_id_type=MESH)
     for copy in small[0:4]:
         copy.wait()
     pack(elem_ref, count_ref, basis_ref, innov_ref, out_ref)
     mine = pl.ds(pl.multiple_of(me * 8, 8), USED)
-    got_ref[mine, :] = out_ref[mine, :]
+    got_ref[0:USED, :] = out_ref[mine, :]
     pl.semaphore_wait(barrier, GX + GY - 2)
     for peer in column_peers:
         pl.semaphore_signal(all_in, inc=1, device_id=peer, device_id_type=MESH)
 
-    def send(peer):
+    def send(peer, slot):
         to = peer[0] * GY + peer[1]
         pltpu.make_async_remote_copy(
             src_ref=out_ref.at[pl.ds(pl.multiple_of(to * 8, 8), USED)],
-            dst_ref=got_ref.at[mine],
+            dst_ref=got_ref.at[pl.ds(pl.multiple_of(slot * 8, 8), USED)],
             send_sem=far_sem.at[0],
-            recv_sem=far_sem.at[1],
+            recv_sem=far_sem.at[1 + slot // PART],
             device_id=peer,
             device_id_type=MESH,
         ).start()
 
-    for peer in row_peers + column_peers:
-        send(peer)
+    for k, peer in enumerate(row_peers + column_peers):
+        send(peer, k + 1)
     for copy in small[4:]:
         copy.wait()
     operator = trace_ref[...]
@@ -271,19 +274,21 @@
 
     def begin_and_send(c, carry):
         for u in range(share):
-            k = ((c - 1) * share + u) * 52 % far
-            send(((px + 1 + k // (GY - 1)) % GX, (py + 1 + k % (GY - 1)) % GY))
+            turn = (c - 1) * share + u
+            k = turn * 52 % far
+            peer = ((px + 1 + k // (GY - 1)) % GX, (py + 1 + k % (GY - 1)) % GY)
+            send(peer, GX + GY - 1 + turn)
         begin(c)
         return carry
 
     begin(0)
     pl.semaphore_wait(all_in, GY - 1)
     lax.fori_loop(1, EX // 8, begin_and_send, 0)
-    rest = pl.ds(0, (DEV - 1) * USED)
-    pltpu.make_async_copy(out_ref.at[rest], out_ref.at[rest], far_sem.at[0]).wait()
-    pltpu.make_async_copy(got_ref.at[rest], got_ref.at[rest], far_sem.at[1]).wait()
-    unpack(got_ref, pay_ref, col_ref, rowid_ref)
-    force(0, pay_ref, col_ref, rowid_ref, force_ref)
+    for part, count in ((0, PART - 1), (1, PART)):
+        some = pl.ds(0, count * USED)
+        pltpu.make_async_copy(got_ref.at[some], got_ref.at[some], far_sem.at[1 + part]).wait()
+        unpack(part, got_ref, pay_ref, col_ref, rowid_ref)
+        force(0, (part,), pay_ref, col_ref, rowid_ref, force_ref)
 
     peers = (
         (lax.rem(px + GX - 1, GX), py),
@@ -316,12 +321,11 @@
             copies[-1].start()
         return copies
 
-    def take_halos(s, near_ref, copies):
+    def take_halos(s, copies):
         for copy in copies:
             copy.wait()
-        below = jnp.where(py == 0, ysend[s, 0], yrecv[s, 0])
-        above = jnp.where(py == GY - 1, ysend[s, 1], yrecv[s, 1])
-        patch(near_ref, below, above)
+        rim_ref[0] = jnp.where(py == 0, ysend[s, 0], yrecv[s, 0])
+        rim_ref[1] = jnp.where(py == GY - 1, ysend[s, 1], yrecv[s, 1])
 
     def correct_traces(x, carry):
         tr = dot(c_ref[STATE : STATE + 4 * FN, :], triple(force_ref[0, x]))
@@ -332,7 +336,7 @@
         return carry
 
     def middle(x, carry):
-        value = finish(x, acc_ref, near1_ref, b_ref, scale_ref)
+        value = finish(x, acc_ref, near1_ref, rim_ref, b_ref, scale_ref)
         hi, lo = split(rows(value[0:NODES] + force_ref[1, x], value[NODES:STATE]))
         slab[x, 0:STATE, :] = hi
         slab[x, STATE : 2 * STATE, :] = lo
@@ -350,16 +354,18 @@
     down, up = lax.fori_loop(0, EX, correct_traces, (rim, rim), unroll=16)
     copies = send_halos(0, near1_ref, down, up)
     lax.fori_loop(0, EX, correct, 0, unroll=16)
-    force(1, pay_ref, col_ref, rowid_ref, force_ref)
-    take_halos(0, near1_ref, copies)
+    force(1, (0, 1), pay_ref, col_ref, rowid_ref, force_ref)
+    take_halos(0, copies)
     lax.fori_loop(0, EX, middle, 0, unroll=16)
     down, up = lax.fori_loop(0, EX, trace, (rim, rim), unroll=16)
     copies = send_halos(1, near2_ref, down, up)
     lax.fori_loop(0, EX, hold, 0, unroll=16)
-    take_halos(1, near2_ref, copies)
-
-
-def last_kernel(acc_ref, near_ref, b_ref, scale_ref, out_ref, stage, sem):
+    take_halos(1, copies)
+    rest = pl.ds(0, (DEV - 1) * USED)
+    pltpu.make_async_copy(out_ref.at[rest], out_ref.at[rest], far_sem.at[0]).wait()
+
+
+def last_kernel(acc_ref, near_ref, rim_ref, b_ref, scale_ref, out_ref, stage, sem):
     def store(c, h):
         band = pl.ds(pl.multiple_of(c * 8, 8), 8)
         column = slice(h * 128, h * 128 + 128)
@@ -371,7 +377,7 @@
 
     def body(c, carry):
         for r in range(8):
-            value = finish(c * 8 + r, acc_ref, near_ref, b_ref, scale_ref)
+            value = finish(c * 8 + r, acc_ref, near_ref, rim_ref, b_ref, scale_ref)
             for h in range(2):
                 flat[row(c, h, r), :] = value[:, h * 128 : h * 128 + 128]
         for h in range(2):
@@ -388,16 +394,17 @@
     adjoint_state, inverse_scale, element_inverse, trace_op, lift_op,
     obs_elem, obs_count, obs_basis, innovation,
 ):
-    acc, near, lift, scale = pl.pallas_call(
+    acc, near, rim, lift, scale = pl.pallas_call(
         main_kernel,
         out_shape=(
             pltpu.VMEM((EX, STATE, EY), F32),
             pltpu.VMEM((EX + 2, 4 * FN, EY), F32),
+            pltpu.VMEM((2, FN, 128), F32),
             pltpu.VMEM((STATE, 12 * FN), BF),
             pltpu.VMEM((EX, EY), F32),
         ),
         in_specs=[HBM] * 9,
-        out_specs=(VMEM, VMEM, VMEM, VMEM),
+        out_specs=(VMEM,) * 5,
         scratch_shapes=[
             pltpu.VMEM((EX // 4 * STATE, 8, 128), F32),
             pltpu.VMEM((EX, 2 * STATE, EY), BF),
@@ -422,7 +429,7 @@
             pltpu.VMEM((STEPS, 2, FN, 128), F32),
             pltpu.SemaphoreType.DMA((EX // 8, 2)),
             pltpu.SemaphoreType.DMA((8,)),
-            pltpu.SemaphoreType.DMA((2,)),
+            pltpu.SemaphoreType.DMA((3,)),
             pltpu.SemaphoreType.DMA((STEPS, 4)),
             pltpu.SemaphoreType.DMA((STEPS, 4)),
             pltpu.SemaphoreType.REGULAR,
@@ -443,7 +450,7 @@
     return pl.pallas_call(
         last_kernel,
         out_shape=jax.ShapeDtypeStruct((STATE, EX, EY), F32),
-        in_specs=[VMEM, VMEM, VMEM, VMEM],
+        in_specs=[VMEM] * 5,
         out_specs=HBM,
         scratch_shapes=[
             pltpu.VMEM((EX // 4 * STATE, 8, 128), F32),
@@ -451,7 +458,7 @@
         ],
         compiler_params=pltpu.CompilerParams(vmem_limit_bytes=24 << 20),
         name="last",
-    )(acc, near, lift, scale)
+    )(acc, near, rim, lift, scale)
 
 
 def solution(mesh):

time: 42.6 us -> 42.1 us (0.988)
  Pallas kernels: 42.3 us -> 41.8 us
    pallas_call x1, Pallas kernels: 38.5 us -> 37.7 us  [local(): pl.pallas_call(main_kernel, out_shape=(pltpu.VMEM((EX, STATE, EY), F32),...]
where the time goes in v3:
time: 42.1 us; the launch traced here: 42 us
  Pallas kernels  41.8 us (99%)
    pallas_call x1, Pallas kernels, local(): pl.pallas_call(main_kernel, out_shape=(pltpu.VMEM((EX, STATE, EY), F32),...  37.7 us
    pallas_call x1, Pallas kernels, local(): pl.pallas_call(last_kernel, out_shape=jax.ShapeDtypeStruct((STATE, EX, EY...  4.15 us

profile of v3, /device:TPU:1, one launch (start us, length us, event | category | flops | bytes accessed | tf_op | source)
XLA Modules:
  0.0 42.0 jit_solution(16782452313023349822)
XLA Ops:
  0.0 37.7 %main.1 = (f32[32,192,256]{2,1,0:T(8,128)S(1)}, f32[34,96,256]{2,1,0:T(8,128)S(1)}, f32[2,24,128]{2,1,0:T(8,128)S(1)}, bf16[192,288]{1,0:T(8,128)(2,1)S(1)}, f32[32,256]{1,0:T(8,128)S(1)}) custom-call(f32[192,32,256]{2,1,0:T(8,128)} %state_hbm.1, f32[32,256]{1,0:T(8,128)} %scale_hbm.1, f32[192,192]{1,0:T(8,128)} %inverse_hbm.1, f32[96,192]{1,0:T(8,128)} %trace_hbm.1, ...), custom_call_target="tpu_custom_call" | custom-call | tf_op jit(solution)/shard_map/main/pallas_call | solution.py:397
  37.7 4.2 %last.1 = f32[192,32,256]{2,1,0:T(8,128)} custom-call(f32[32,192,256]{2,1,0:T(8,128)S(1)} %get-tuple-element.10.acc_ref, f32[34,96,256]{2,1,0:T(8,128)S(1)} %get-tuple-element.11.near_ref, f32[2,24,128]{2,1,0:T(8,128)S(1)} %get-tuple-element.12.rim_ref, bf16[192,288]{1,0:T(8,128)(2,1)S(1)} %get-tuple-element.13.b_ref, f32[32,256]{1,0:T(8,128)S(1)} %get-tuple-element.14.scale_ref), custom_call_target="tpu_custom_call" | custom-call | tf_op jit(solution)/shard_map/last/pallas_call | solution.py:450

commit v4 on v3

--- a/solution.py
+++ b/solution.py
@@ -58,10 +58,13 @@
     return rows(hi, lo, hi)
 
 
-def weights(v):
-    hi, lo = split(v)
-    hi, lo = hi.astype(F32), lo.astype(F32)
-    return lanes(hi, hi, lo).astype(BF)
+def weights(*values):
+    parts = []
+    for v in values:
+        hi, lo = split(v)
+        hi, lo = hi.astype(F32), lo.astype(F32)
+        parts += [hi, hi, lo]
+    return lanes(*parts).astype(BF)
 
 
 def tile(c, h):
@@ -177,7 +180,7 @@
     return down, up
 
 
-def finish(x, acc_ref, near_ref, rim_ref, b_ref, scale_ref):
+def finish(x, acc_ref, near_ref, rim_ref, b_ref, scale_ref, force=None):
     lane = iota((FN, 128), 1)
     below = pltpu.roll(rim_ref[0], (128 - x) % 128, 1)
     above = pltpu.roll(rim_ref[1], 127 - x, 1)
@@ -185,14 +188,17 @@
     south, north = near[2 * FN : 3 * FN], near[3 * FN : 4 * FN]
     south = lanes(jnp.where(lane == 0, below, south[:, 0:128]), south[:, 128:256])
     north = lanes(north[:, 0:128], jnp.where(lane == 127, above, north[:, 128:256]))
-    lifted = dot(b_ref[...], triple(rows(near[0 : 2 * FN], south, north)))
+    given = triple(rows(near[0 : 2 * FN], south, north))
+    if force is not None:
+        given = rows(given, triple(force))
+    lifted = dot(b_ref[...], given)
     return (acc_ref[x] + lifted) * scale_ref[pl.ds(x, 1), :]
 
 
 def main_kernel(
     state_hbm, scale_hbm, inverse_hbm, trace_hbm, lift_hbm, elem_hbm, count_hbm, basis_hbm, innov_hbm,
     acc_ref, near2_ref, rim_ref, b_ref, scale_ref,
-    stage, slab, near1_ref, tr_ref, force_ref, pay_ref, col_ref, rowid_ref, at_ref, c_ref,
+    stage, slab, near1_ref, tr_ref, force_ref, pay_ref, col_ref, rowid_ref, at_ref, c_ref, bc_ref, t_ref,
     inverse_ref, trace_ref, lift_ref, elem_ref, count_ref, basis_ref, innov_ref,
     out_ref, got_ref, ysend, yrecv,
     load_sem, small_sem, far_sem, near_send, near_recv, all_in,
@@ -254,7 +260,11 @@
     half = 0.5 * dot_full(inverse, lift_ref[...])
     whole = inverse + dot_full(half, operator)
     at_ref[...] = weights(rows(whole, operator))
-    c_ref[...] = weights(rows(whole, operator)[:, 0:NODES])
+    c_ref[...] = weights(operator[:, 0:NODES])
+    bc_ref[...] = weights(half, whole[:, 0:NODES])
+    hi, lo = split(operator)
+    t_ref[0 : 4 * FN, :] = hi
+    t_ref[4 * FN : 8 * FN, :] = lo
     b_ref[...] = weights(half)
 
     flat = stage.reshape(EX // 4 * STATE * 8, 128)
@@ -328,38 +338,36 @@
         rim_ref[1] = jnp.where(py == GY - 1, ysend[s, 1], yrecv[s, 1])
 
     def correct_traces(x, carry):
-        tr = dot(c_ref[STATE : STATE + 4 * FN, :], triple(force_ref[0, x]))
+        tr = dot(c_ref[...], triple(force_ref[0, x]))
         return put(x, tr_ref[x] + tr, near1_ref, carry)
 
-    def correct(x, carry):
-        acc_ref[x] += dot(c_ref[0:STATE, :], triple(force_ref[0, x]))
-        return carry
-
     def middle(x, carry):
-        value = finish(x, acc_ref, near1_ref, rim_ref, b_ref, scale_ref)
+        value = finish(
+            x, acc_ref, near1_ref, rim_ref, bc_ref, scale_ref, force_ref[0, x]
+        )
         hi, lo = split(rows(value[0:NODES] + force_ref[1, x], value[NODES:STATE]))
         slab[x, 0:STATE, :] = hi
         slab[x, STATE : 2 * STATE, :] = lo
         return carry
 
     def trace(x, carry):
-        tr = dot(at_ref[STATE : STATE + 4 * FN, :], rows(slab[x], slab[x, 0:STATE, :]))
-        return put(x, tr, near2_ref, carry)
+        both = dot(t_ref[...], slab[x, 0:STATE, :])
+        tr = dot(t_ref[0 : 4 * FN, :], slab[x, STATE : 2 * STATE, :])
+        return put(x, both[0 : 4 * FN] + both[4 * FN : 8 * FN] + tr, near2_ref, carry)
 
     def hold(x, carry):
         acc_ref[x] = dot(at_ref[0:STATE, :], rows(slab[x], slab[x, 0:STATE, :]))
         return carry
 
     rim = jnp.zeros((FN, 128), F32)
-    down, up = lax.fori_loop(0, EX, correct_traces, (rim, rim), unroll=16)
+    down, up = lax.fori_loop(0, EX, correct_traces, (rim, rim), unroll=32)
     copies = send_halos(0, near1_ref, down, up)
-    lax.fori_loop(0, EX, correct, 0, unroll=16)
     force(1, (0, 1), pay_ref, col_ref, rowid_ref, force_ref)
     take_halos(0, copies)
-    lax.fori_loop(0, EX, middle, 0, unroll=16)
-    down, up = lax.fori_loop(0, EX, trace, (rim, rim), unroll=16)
+    lax.fori_loop(0, EX, middle, 0, unroll=32)
+    down, up = lax.fori_loop(0, EX, trace, (rim, rim), unroll=32)
     copies = send_halos(1, near2_ref, down, up)
-    lax.fori_loop(0, EX, hold, 0, unroll=16)
+    lax.fori_loop(0, EX, hold, 0, unroll=32)
     take_halos(1, copies)
     rest = pl.ds(0, (DEV - 1) * USED)
     pltpu.make_async_copy(out_ref.at[rest], out_ref.at[rest], far_sem.at[0]).wait()
@@ -415,7 +423,9 @@
             pltpu.VMEM((STEPS, 2 * OBS, EY), BF),
             pltpu.VMEM((8, OBS), jnp.int32),
             pltpu.VMEM((STATE + 4 * FN, 3 * STATE), BF),
-            pltpu.VMEM((STATE + 4 * FN, 3 * NODES), BF),
+            pltpu.VMEM((4 * FN, 3 * NODES), BF),
+            pltpu.VMEM((STATE, 12 * FN + 3 * NODES), BF),
+            pltpu.VMEM((8 * FN, STATE), BF),
             pltpu.VMEM((STATE, STATE), F32),
             pltpu.VMEM((4 * FN, STATE), F32),
             pltpu.VMEM((STATE, 4 * FN), F32),

time: 42.1 us -> 41.3 us (0.981)
  Pallas kernels: 41.8 us -> 41 us
    pallas_call x1, Pallas kernels: 37.7 us -> 36.9 us  [local(): pl.pallas_call(main_kernel, out_shape=(pltpu.VMEM((EX, STATE, EY), F32),...]
where the time goes in v4:
time: 41.3 us; the launch traced here: 41.2 us
  Pallas kernels  41 us (99%)
    pallas_call x1, Pallas kernels, local(): pl.pallas_call(main_kernel, out_shape=(pltpu.VMEM((EX, STATE, EY), F32),...  36.9 us
    pallas_call x1, Pallas kernels, local(): pl.pallas_call(last_kernel, out_shape=jax.ShapeDtypeStruct((STATE, EX, EY...  4.15 us

profile of v4, /device:TPU:1, one launch (start us, length us, event | category | flops | bytes accessed | tf_op | source)
XLA Modules:
  0.0 41.2 jit_solution(2064154442639997201)
XLA Ops:
  0.0 36.9 %main.1 = (f32[32,192,256]{2,1,0:T(8,128)S(1)}, f32[34,96,256]{2,1,0:T(8,128)S(1)}, f32[2,24,128]{2,1,0:T(8,128)S(1)}, bf16[192,288]{1,0:T(8,128)(2,1)S(1)}, f32[32,256]{1,0:T(8,128)S(1)}) custom-call(f32[192,32,256]{2,1,0:T(8,128)} %state_hbm.1, f32[32,256]{1,0:T(8,128)} %scale_hbm.1, f32[192,192]{1,0:T(8,128)} %inverse_hbm.1, f32[96,192]{1,0:T(8,128)} %trace_hbm.1, ...), custom_call_target="tpu_custom_call" | custom-call | tf_op jit(solution)/shard_map/main/pallas_call | solution.py:405
  36.9 4.2 %last.1 = f32[192,32,256]{2,1,0:T(8,128)} custom-call(f32[32,192,256]{2,1,0:T(8,128)S(1)} %get-tuple-element.10.acc_ref, f32[34,96,256]{2,1,0:T(8,128)S(1)} %get-tuple-element.11.near_ref, f32[2,24,128]{2,1,0:T(8,128)S(1)} %get-tuple-element.12.rim_ref, bf16[192,288]{1,0:T(8,128)(2,1)S(1)} %get-tuple-element.13.b_ref, f32[32,256]{1,0:T(8,128)S(1)} %get-tuple-element.14.scale_ref), custom_call_target="tpu_custom_call" | custom-call | tf_op jit(solution)/shard_map/last/pallas_call | solution.py:460

commit v5 on v4

--- a/solution.py
+++ b/solution.py
@@ -280,20 +280,20 @@
             tr_ref[x] = both[STATE:]
 
     far = (GX - 1) * (GY - 1)
-    share = far // (EX // 8 - 1)
-
-    def begin_and_send(c, carry):
-        for u in range(share):
-            turn = (c - 1) * share + u
-            k = turn * 52 % far
-            peer = ((px + 1 + k // (GY - 1)) % GX, (py + 1 + k % (GY - 1)) % GY)
-            send(peer, GX + GY - 1 + turn)
-        begin(c)
+    def push(turn, carry):
+        peer = ((px + 1 + turn // (GY - 1)) % GX, (py + 1 + turn % (GY - 1)) % GY)
+        send(peer, GX + GY - 1 + turn)
         return carry
 
     begin(0)
     pl.semaphore_wait(all_in, GY - 1)
-    lax.fori_loop(1, EX // 8, begin_and_send, 0)
+    lax.fori_loop(0, far, push, 0, unroll=7)
+
+    def begin_more(c, carry):
+        begin(c)
+        return carry
+
+    lax.fori_loop(1, EX // 8, begin_more, 0)
     for part, count in ((0, PART - 1), (1, PART)):
         some = pl.ds(0, count * USED)
         pltpu.make_async_copy(got_ref.at[some], got_ref.at[some], far_sem.at[1 + part]).wait()

time: 41.3 us -> 40 us (0.969)
  Pallas kernels: 41 us -> 39.4 us
    pallas_call x1, Pallas kernels: 36.9 us -> 35.2 us  [local(): pl.pallas_call(main_kernel, out_shape=(pltpu.VMEM((EX, STATE, EY), F32),...]
where the time goes in v5:
time: 40 us; the launch traced here: 39.5 us
  Pallas kernels  39.4 us (98%)
    pallas_call x1, Pallas kernels, local(): pl.pallas_call(main_kernel, out_shape=(pltpu.VMEM((EX, STATE, EY), F32),...  35.2 us
    pallas_call x1, Pallas kernels, local(): pl.pallas_call(last_kernel, out_shape=jax.ShapeDtypeStruct((STATE, EX, EY...  4.15 us

profile of v5, /device:TPU:1, one launch (start us, length us, event | category | flops | bytes accessed | tf_op | source)
XLA Modules:
  0.0 39.5 jit_solution(3956735321561365917)
XLA Ops:
  0.0 35.2 %main.1 = (f32[32,192,256]{2,1,0:T(8,128)S(1)}, f32[34,96,256]{2,1,0:T(8,128)S(1)}, f32[2,24,128]{2,1,0:T(8,128)S(1)}, bf16[192,288]{1,0:T(8,128)(2,1)S(1)}, f32[32,256]{1,0:T(8,128)S(1)}) custom-call(f32[192,32,256]{2,1,0:T(8,128)} %state_hbm.1, f32[32,256]{1,0:T(8,128)} %scale_hbm.1, f32[192,192]{1,0:T(8,128)} %inverse_hbm.1, f32[96,192]{1,0:T(8,128)} %trace_hbm.1, ...), custom_call_target="tpu_custom_call" | custom-call | tf_op jit(solution)/shard_map/main/pallas_call | solution.py:405
  35.2 4.2 %last.1 = f32[192,32,256]{2,1,0:T(8,128)} custom-call(f32[32,192,256]{2,1,0:T(8,128)S(1)} %get-tuple-element.10.acc_ref, f32[34,96,256]{2,1,0:T(8,128)S(1)} %get-tuple-element.11.near_ref, f32[2,24,128]{2,1,0:T(8,128)S(1)} %get-tuple-element.12.rim_ref, bf16[192,288]{1,0:T(8,128)(2,1)S(1)} %get-tuple-element.13.b_ref, f32[32,256]{1,0:T(8,128)S(1)} %get-tuple-element.14.scale_ref), custom_call_target="tpu_custom_call" | custom-call | tf_op jit(solution)/shard_map/last/pallas_call | solution.py:460

commit v6 on v5

--- a/solution.py
+++ b/solution.py
@@ -392,7 +392,7 @@
             store(c, h).start()
         return carry
 
-    lax.fori_loop(0, EX // 8, body, 0)
+    lax.fori_loop(0, EX // 8, body, 0, unroll=True)
     for c in range(EX // 8):
         for h in range(2):
             store(c, h).wait()

time: 40 us -> 39.2 us (0.980)
  Pallas kernels: 39.4 us -> 38.7 us
    pallas_call x1, Pallas kernels: 4.15 us -> 3.51 us  [local(): pl.pallas_call(last_kernel, out_shape=jax.ShapeDtypeStruct((STATE, EX, EY...]
where the time goes in v6:
time: 39.2 us; the launch traced here: 38.9 us
  Pallas kernels  38.7 us (99%)
    pallas_call x1, Pallas kernels, local(): pl.pallas_call(main_kernel, out_shape=(pltpu.VMEM((EX, STATE, EY), F32),...  35.2 us
    pallas_call x1, Pallas kernels, local(): pl.pallas_call(last_kernel, out_shape=jax.ShapeDtypeStruct((STATE, EX, EY...  3.51 us

profile of v6, /device:TPU:1, one launch (start us, length us, event | category | flops | bytes accessed | tf_op | source)
XLA Modules:
  0.0 38.9 jit_solution(1305964269042935064)
XLA Ops:
  0.0 35.2 %main.1 = (f32[32,192,256]{2,1,0:T(8,128)S(1)}, f32[34,96,256]{2,1,0:T(8,128)S(1)}, f32[2,24,128]{2,1,0:T(8,128)S(1)}, bf16[192,288]{1,0:T(8,128)(2,1)S(1)}, f32[32,256]{1,0:T(8,128)S(1)}) custom-call(f32[192,32,256]{2,1,0:T(8,128)} %state_hbm.1, f32[32,256]{1,0:T(8,128)} %scale_hbm.1, f32[192,192]{1,0:T(8,128)} %inverse_hbm.1, f32[96,192]{1,0:T(8,128)} %trace_hbm.1, ...), custom_call_target="tpu_custom_call" | custom-call | tf_op jit(solution)/shard_map/main/pallas_call | solution.py:405
  35.2 3.5 %last.1 = f32[192,32,256]{2,1,0:T(8,128)} custom-call(f32[32,192,256]{2,1,0:T(8,128)S(1)} %get-tuple-element.10.acc_ref, f32[34,96,256]{2,1,0:T(8,128)S(1)} %get-tuple-element.11.near_ref, f32[2,24,128]{2,1,0:T(8,128)S(1)} %get-tuple-element.12.rim_ref, bf16[192,288]{1,0:T(8,128)(2,1)S(1)} %get-tuple-element.13.b_ref, f32[32,256]{1,0:T(8,128)S(1)} %get-tuple-element.14.scale_ref), custom_call_target="tpu_custom_call" | custom-call | tf_op jit(solution)/shard_map/last/pallas_call | solution.py:460

commit v7 on v6

--- a/solution.py
+++ b/solution.py
@@ -163,7 +163,7 @@
             force_ref[s, g * group + i] = mine
         return carry
 
-    lax.fori_loop(0, EX // group, body, 0)
+    lax.fori_loop(0, EX // group, body, 0, unroll=True)
 
 
 def put(x, tr, near_ref, carry):
@@ -293,7 +293,7 @@
         begin(c)
         return carry
 
-    lax.fori_loop(1, EX // 8, begin_more, 0)
+    lax.fori_loop(1, EX // 8, begin_more, 0, unroll=True)
     for part, count in ((0, PART - 1), (1, PART)):
         some = pl.ds(0, count * USED)
         pltpu.make_async_copy(got_ref.at[some], got_ref.at[some], far_sem.at[1 + part]).wait()

time: 39.2 us -> 38.2 us (0.974)
  Pallas kernels: 38.7 us -> 37.7 us
    pallas_call x1, Pallas kernels: 35.2 us -> 34.2 us  [local(): pl.pallas_call(main_kernel, out_shape=(pltpu.VMEM((EX, STATE, EY), F32),...]
where the time goes in v7:
time: 38.2 us; the launch traced here: 37.9 us
  Pallas kernels  37.7 us (99%)
    pallas_call x1, Pallas kernels, local(): pl.pallas_call(main_kernel, out_shape=(pltpu.VMEM((EX, STATE, EY), F32),...  34.2 us
    pallas_call x1, Pallas kernels, local(): pl.pallas_call(last_kernel, out_shape=jax.ShapeDtypeStruct((STATE, EX, EY...  3.51 us

profile of v7, /device:TPU:1, one launch (start us, length us, event | category | flops | bytes accessed | tf_op | source)
XLA Modules:
  0.0 37.9 jit_solution(9293008035957592422)
XLA Ops:
  0.0 34.2 %main.1 = (f32[32,192,256]{2,1,0:T(8,128)S(1)}, f32[34,96,256]{2,1,0:T(8,128)S(1)}, f32[2,24,128]{2,1,0:T(8,128)S(1)}, bf16[192,288]{1,0:T(8,128)(2,1)S(1)}, f32[32,256]{1,0:T(8,128)S(1)}) custom-call(f32[192,32,256]{2,1,0:T(8,128)} %state_hbm.1, f32[32,256]{1,0:T(8,128)} %scale_hbm.1, f32[192,192]{1,0:T(8,128)} %inverse_hbm.1, f32[96,192]{1,0:T(8,128)} %trace_hbm.1, ...), custom_call_target="tpu_custom_call" | custom-call | tf_op jit(solution)/shard_map/main/pallas_call | solution.py:405
  34.2 3.5 %last.1 = f32[192,32,256]{2,1,0:T(8,128)} custom-call(f32[32,192,256]{2,1,0:T(8,128)S(1)} %get-tuple-element.10.acc_ref, f32[34,96,256]{2,1,0:T(8,128)S(1)} %get-tuple-element.11.near_ref, f32[2,24,128]{2,1,0:T(8,128)S(1)} %get-tuple-element.12.rim_ref, bf16[192,288]{1,0:T(8,128)(2,1)S(1)} %get-tuple-element.13.b_ref, f32[32,256]{1,0:T(8,128)S(1)} %get-tuple-element.14.scale_ref), custom_call_target="tpu_custom_call" | custom-call | tf_op jit(solution)/shard_map/last/pallas_call | solution.py:460
